TPU v7x, 32 devices: a whole 2x2x4 slice. The times are simulated.
32 devices in a mesh: groups: 2 (over y), seq: 4 (over x, core), heads: 4 (over z).
Axes of the slice: x: 2, y: 2, z: 4, core: 2. Of those that a mesh axis runs over, the one named last changes fastest.
Arguments:
- final_state: bfloat16 [2, 32, 1, 64, 80, 128], P(None, ('groups', 'seq', 'heads')), parts along dimension 1, may hold values from -2 to 2
- channel_tail: bfloat16 [2, 32, 1, 3, 5120], P(None, ('groups', 'seq', 'heads')), parts along dimension 1, may hold values from -6 to 6
- matrix_tail: bfloat16 [32, 1, 2, 3, 256], P(('groups', 'seq', 'heads')), parts along dimension 0, may hold values from -6 to 6
- last_hidden: bfloat16 [32, 1, 5120], P(('groups', 'seq', 'heads')), parts along dimension 0, may hold values from -6 to 6
- decode_group: int32 [32, 1], P(('groups', 'seq')), parts along dimension 0, may hold values from 0 to 3; in each aligned block of 4 rows (0 to 3, 4 to 7, ...) at most 2 rows name the same one
- input_weight: bfloat16 [2, 5120, 2, 5120], P(None, 'seq', None, 'heads'), may hold values from -0.078125 to 0.078125
- step_weight: bfloat16 [2, 5120, 64], P(None, 'seq', 'heads'), may hold values from -0.078125 to 0.078125
- matrix_weight: bfloat16 [2, 5120, 256], P(None, 'seq'), may hold values from -0.078125 to 0.078125
- channel_conv: float32 [2, 4, 5120], P(None, None, 'heads'), may hold values from -3 to 3
- matrix_conv: float32 [2, 4, 256], replicated, may hold values from -3 to 3
- step_bias: float32 [2, 64], P(None, 'heads'), may hold values from -4 to -1
- decay_log: float32 [2, 64], P(None, 'heads'), may hold values from 0 to 2.8
- skip_gain: float32 [2, 64], P(None, 'heads'), may hold values from 0.5 to 2
- norm_gain: float32 [2, 5120], P(None, 'heads'), may hold values from 0.25 to 1.75
- output_weight: bfloat16 [2, 5120, 5120], P(None, 'heads', 'seq'), may hold values from -0.078125 to 0.078125
Outputs:
- decoded: bfloat16 [64, 5120], P(('groups', 'heads'), 'seq'), parts along dimension 0
- new_state: bfloat16 [2, 8, 8, 64, 80, 128], P(None, ('groups', 'seq'), None, 'heads'), parts along dimension 1
There are 2 independent parts, one for each index of `groups`. A program takes and returns all parts, laid end to end along the dimension named above; an argument that names none is the same for every part. Nothing has to cross between parts.
Inputs may be any that keep to these rules, and one draw needn't show every extreme that they name: `decode_group`: in each aligned block of 4 rows (the requests of one prefill row) no group is named more than 2 times; some group is named exactly 2 times in some block.
All inputs are finite; a program needn't handle non-finite values.
Results may differ from a plain program's by a relative error of at most 0.0065.
Values may be sent and summed in bfloat16 or wider, within the bound.
A program may use at most 128 MiB of HBM per device.

v0:
```python
import jax
import jax.numpy as jnp
from jax import lax
from jax.sharding import PartitionSpec as P

epsilon = 1e-05


def convolve(tail_block, taps_weight, fresh):
    kernel_taps = taps_weight.shape[0]
    summed = taps_weight[kernel_taps - 1] * fresh
    for tap_index in range(kernel_taps - 1):
        summed = summed + taps_weight[tap_index] * tail_block[:, tap_index].astype(jnp.float32)
    return jax.nn.silu(summed)


def on_device(
    final_state,
    channel_tail,
    matrix_tail,
    last_hidden,
    decode_group,
    input_weight,
    step_weight,
    matrix_weight,
    channel_conv,
    matrix_conv,
    step_bias,
    decay_log,
    skip_gain,
    norm_gain,
    output_weight,
):
    heads_count = lax.axis_size("heads")
    seq_count = lax.axis_size("seq")
    layers = final_state.shape[0]
    slot_count = final_state.shape[2]
    heads_all = final_state.shape[3]
    head_width = final_state.shape[4]
    state_width = final_state.shape[5]
    head_dev = heads_all // heads_count
    model_width = last_hidden.shape[2]
    kernel_taps = channel_conv.shape[1]
    members = heads_count * slot_count
    pair_cap = 2 * slot_count * heads_count // seq_count
    capacity = seq_count * pair_cap
    rows_total = capacity * seq_count
    share_rows = rows_total // heads_count
    dev_channels = head_dev * head_width
    flat_state = head_width * state_width
    dest_group = decode_group[:, 0]
    member_ids = jnp.arange(members, dtype=jnp.int32)
    earlier = (dest_group[:, None] == dest_group[None, :]) & (
        member_ids[None, :] < member_ids[:, None]
    )
    group_rank = jnp.sum(earlier.astype(jnp.int32), axis=1)
    target = dest_group * pair_cap + group_rank
    buffer_ids = jnp.arange(capacity, dtype=jnp.int32)
    matches = target[None, :] == buffer_ids[:, None]
    source = jnp.sum(jnp.where(matches, member_ids[None, :], 0), axis=1)
    filled = jnp.any(matches, axis=1)

    def select_rows(array, axis_pos):
        taken = jnp.take(array, source, axis=axis_pos)
        shape_mask = [1] * array.ndim
        shape_mask[axis_pos] = capacity
        return jnp.where(filled.reshape(shape_mask), taken, jnp.zeros((), array.dtype))

    row_hidden, row_matrix = (
        lax.all_gather(last_hidden, "heads", axis=0, tiled=True),
        lax.all_gather(matrix_tail, "heads", axis=0, tiled=True),
    )
    send_hidden = select_rows(row_hidden.reshape(members, model_width), 0)
    send_matrix = select_rows(row_matrix.reshape(members, -1), 0)
    state_send = final_state.reshape(layers, 1, slot_count, 1, heads_all, flat_state)
    tail_send = channel_tail.reshape(layers, 1, slot_count, kernel_taps - 1, heads_all, head_width)
    state_heads, tail_heads = (
        lax.all_to_all(state_send, "heads", split_axis=4, concat_axis=1, tiled=True),
        lax.all_to_all(tail_send, "heads", split_axis=4, concat_axis=1, tiled=True),
    )
    state_heads = state_heads.reshape(layers, members, head_dev, flat_state)
    tail_heads = tail_heads.reshape(layers, members, kernel_taps - 1, dev_channels)
    joint_states, joint_tails, matrix_recv, hidden_recv = (
        lax.all_to_all(select_rows(state_heads, 1), "seq", split_axis=1, concat_axis=1, tiled=True),
        lax.all_to_all(select_rows(tail_heads, 1), "seq", split_axis=1, concat_axis=1, tiled=True),
        lax.all_to_all(send_matrix[None], "seq", split_axis=1, concat_axis=1, tiled=True),
        lax.all_to_all(send_hidden[None], "seq", split_axis=1, concat_axis=1, tiled=True),
    )
    matrix_recv = matrix_recv[0]
    hidden_recv = hidden_recv[0]
    new_states = []
    current = None
    result = None
    for layer_index in range(layers):
        state_in = joint_states[layer_index]
        tail_in = joint_tails[layer_index]
        if layer_index == 0:
            current = lax.all_to_all(hidden_recv, "seq", split_axis=1, concat_axis=0, tiled=True)
        width_piece = current.shape[1]
        weight_in = input_weight[layer_index].reshape(width_piece, 2 * dev_channels)
        weight_step = step_weight[layer_index]
        weight_matrix = matrix_weight[layer_index]
        row_block = current
        projected = lax.psum_scatter(
            jnp.concatenate(
                [
                    jnp.dot(row_block, weight_in, preferred_element_type=jnp.float32),
                    jnp.dot(row_block, weight_step, preferred_element_type=jnp.float32),
                    jnp.dot(row_block, weight_matrix, preferred_element_type=jnp.float32),
                ],
                axis=1,
            ),
            "seq",
            scatter_dimension=0,
            tiled=True,
        )
        gate_part = projected[:, :dev_channels]
        fresh_x = projected[:, dev_channels : 2 * dev_channels]
        step_raw = projected[:, 2 * dev_channels : 2 * dev_channels + head_dev]
        matrix_raw = projected[:, 2 * dev_channels + head_dev :]
        matrix_tails = matrix_recv.reshape(capacity, layers, kernel_taps - 1, 2 * state_width)
        conv_x = convolve(tail_in, channel_conv[layer_index], fresh_x)
        conv_matrix = convolve(matrix_tails[:, layer_index], matrix_conv[layer_index], matrix_raw)
        input_matrix = conv_matrix[:, :state_width]
        output_matrix = conv_matrix[:, state_width:]
        step_size = jax.nn.softplus(step_raw + step_bias[layer_index])
        decay_rate = jnp.exp(-jnp.exp(decay_log[layer_index]) * step_size)
        head_x = conv_x.reshape(capacity, head_dev, head_width)
        old_state = state_in.reshape(capacity, head_dev, head_width, state_width).astype(
            jnp.float32
        )
        fresh_state = (
            decay_rate[:, :, None, None] * old_state
            + (step_size[:, :, None] * head_x)[:, :, :, None] * input_matrix[:, None, None, :]
        )
        read_out = jnp.einsum(
            "rhpn,rn->rhp", fresh_state, output_matrix, precision=lax.Precision.HIGHEST
        )
        new_states.append(fresh_state.astype(jnp.bfloat16))
        y_heads = read_out + skip_gain[layer_index][None, :, None] * head_x
        gated = y_heads.reshape(capacity, dev_channels) * jax.nn.silu(gate_part)
        sum_sq = lax.psum(jnp.sum(gated * gated, axis=1), "heads")
        normed = (
            gated
            * lax.rsqrt(sum_sq[:, None] / (heads_all * head_width) + epsilon)
            * norm_gain[layer_index]
        ).astype(jnp.bfloat16)
        mixed_all = lax.all_gather(normed, "seq", axis=0, tiled=True)
        weight_out = output_weight[layer_index]
        out_term = lax.psum_scatter(
            jnp.dot(mixed_all, weight_out, preferred_element_type=jnp.float32),
            "heads",
            scatter_dimension=0,
            tiled=True,
        )
        residual = lax.dynamic_slice_in_dim(
            current, lax.axis_index("heads") * share_rows, share_rows, 0
        )
        result = (residual.astype(jnp.float32) + out_term).astype(jnp.bfloat16)
        if layer_index + 1 < layers:
            current = lax.all_gather(result, "heads", axis=0, tiled=True)
    return (result, jnp.stack(new_states)[:, None])


def solution(mesh):
    return jax.shard_map(
        on_device,
        mesh=mesh,
        in_specs=(
            P(None, ("groups", "seq", "heads"), None, None, None, None),
            P(None, ("groups", "seq", "heads"), None, None, None),
            P(("groups", "seq", "heads"), None, None, None, None),
            P(("groups", "seq", "heads"), None, None),
            P(("groups", "seq"), None),
            P(None, "seq", None, "heads"),
            P(None, "seq", "heads"),
            P(None, "seq", None),
            P(None, None, "heads"),
            P(),
            P(None, "heads"),
            P(None, "heads"),
            P(None, "heads"),
            P(None, "heads"),
            P(None, "heads", "seq"),
        ),
        out_specs=(
            P(("groups", "heads"), "seq"),
            P(None, ("groups", "seq"), None, "heads", None, None),
        ),
        check_vma=False,
    )
```

profile of v0, /device:TPU:0, one launch (start us, length us, event | category | flops | bytes accessed | tf_op | source)
XLA Modules:
  0.0 387.2 jit_solution(12913822137516419175)
XLA Ops:
  8.9 14.8 %all_gather.16 = bf16[4,1,2,3,256]{4,2,3,1,0:T(2,128)(2,1)S(1)} all-gather(bf16[1,1,2,3,256]{4,2,3,1,0:T(2,128)(2,1)} %param.17), channel_id=1, replica_groups=mesh['groups'=2,'seq'=4,'heads'=4] {'heads'}, dimensions={0}, use_global_device_ids=true | all-gather | bytes 15360 | tf_op jit(solution)/shard_map/all_gather | solution.py:71
  29.7 13.5 %all_gather.15 = bf16[4,1,5120]{2,1,0:T(2,128)(2,1)S(1)} all-gather(bf16[1,1,5120]{2,1,0:T(2,128)(2,1)} %param.18), channel_id=1, replica_groups=mesh['groups'=2,'seq'=4,'heads'=4] {'heads'}, dimensions={0}, use_global_device_ids=true | all-gather | bytes 51200 | tf_op jit(solution)/shard_map/all_gather | solution.py:70
  53.3 4.6 %all-to-all-start.4 = ((bf16[2,1,1,3,64,80]{5,0,3,2,1,4:T(2,128)(2,1)}), bf16[2,1,1,3,64,80]{5,0,3,2,1,4:T(2,128)(2,1)S(1)}, u32[]{:S(2)}, u32[]{:S(2)}) async-start(bf16[2,1,1,3,64,80]{5,0,3,2,1,4:T(2,128)(2,1)} %copy.92), calls=%async_computation.4 | async-start | bytes 196608 | tf_op jit(solution)/shard_map/all_to_all | solution.py:79
  61.0 4.2 %copy.109 = bf16[2,1,1,1,64,10240]{5,0,3,2,1,4:T(2,128)(2,1)} copy(bf16[2,1,1,1,64,10240]{5,4,0,3,2,1:T(8,128)(2,1)S(1)} %reshape.357) | data formatting | bytes 5242880 | tf_op jit(solution)/shard_map/reshape | solution.py:75
  65.2 5.1 %all-to-all-start.2 = ((bf16[2,1,1,1,64,10240]{5,0,3,2,1,4:T(2,128)(2,1)}), bf16[2,1,1,1,64,10240]{5,0,3,2,1,4:T(2,128)(2,1)S(1)}, u32[]{:S(2)}, u32[]{:S(2)}) async-start(bf16[2,1,1,1,64,10240]{5,0,3,2,1,4:T(2,128)(2,1)} %copy.109), calls=%async_computation.2 | async-start | bytes 5242880 | tf_op jit(solution)/shard_map/all_to_all | solution.py:78
  70.3 11.5 %fusion.54 = (bf16[1,1280,2,1280]{3,2,1,0:T(2,128)(2,1)}, bf16[1,1280,2,1280]{3,2,1,0:T(2,128)(2,1)S(1)}) fusion(bf16[2,1280,2,1280]{3,2,1,0:T(2,128)(2,1)} %param.20), kind=kLoop, calls=%fused_computation.150 | loop fusion | bytes 26214400 | tf_op jit(solution)/shard_map/slice | solution.py:100
  89.2 39.7 %all-to-all-done.2 = bf16[2,1,1,1,64,10240]{5,0,3,2,1,4:T(2,128)(2,1)S(1)} async-done(((bf16[2,1,1,1,64,10240]{5,0,3,2,1,4:T(2,128)(2,1)}), bf16[2,1,1,1,64,10240]{5,0,3,2,1,4:T(2,128)(2,1)S(1)}, u32[]{:S(2)}, u32[]{:S(2)}) %all-to-all-start.2) | async-done | bytes 2621472 | tf_op jit(solution)/shard_map/all_to_all | solution.py:78
  142.2 5.5 %select_bitcast_fusion = bf16[2,8,16,10240]{3,2,0,1:T(8,128)(2,1)} fusion(bf16[8,2,16,10240]{3,2,1,0:T(8,128)(2,1)} %gather_fusion.1, pred[8]{0:T(512)(128)(4,1)S(1)} %fusion.47, pred[8]{0:T(512)(128)(4,1)S(1)} %compare_and_fusion), kind=kLoop, calls=%fused_computation.11 | loop fusion | flops 5242880 | bytes 10485776 | tf_op jit(solution)/shard_map/jit(_where)/select_n | solution.py:67
  147.8 5.2 %all-to-all-start.3 = ((bf16[2,8,16,10240]{3,2,0,1:T(8,128)(2,1)}), bf16[2,8,16,10240]{3,2,0,1:T(8,128)(2,1)}, u32[]{:S(2)}, u32[]{:S(2)}) async-start(bf16[2,8,16,10240]{3,2,0,1:T(8,128)(2,1)} %select_bitcast_fusion), calls=%async_computation.3 | async-start | bytes 10485760 | tf_op jit(solution)/shard_map/all_to_all | solution.py:84
  159.3 33.8 %all-reduce.5.cloned.1.call-done = f32[32,2832]{1,0:T(8,128)} async-done(((f32[32,2832]{1,0:T(8,128)}), f32[32,2832]{1,0:T(8,128)}) %all-reduce.5.cloned.1.call-update) | async-done | bytes 362512
  195.8 22.9 %all-to-all-done.3 = bf16[2,8,16,10240]{3,2,0,1:T(8,128)(2,1)} async-done(((bf16[2,8,16,10240]{3,2,0,1:T(8,128)(2,1)}), bf16[2,8,16,10240]{3,2,0,1:T(8,128)(2,1)}, u32[]{:S(2)}, u32[]{:S(2)}) %all-to-all-start.3) | async-done | bytes 5242912 | tf_op jit(solution)/shard_map/all_to_all | solution.py:84
  218.7 6.1 %slice_convert_fusion = (f32[1,8,16,10240]{3,2,0,1:T(8,128)}, f32[1,8,16,10240]{3,2,0,1:T(8,128)S(1)}) fusion(bf16[2,8,16,10240]{3,2,0,1:T(8,128)(2,1)} %all-to-all-done.3), kind=kLoop, calls=%fused_computation.22 | loop fusion | flops 2621440 | bytes 15728640 | tf_op jit(solution)/shard_map/convert_element_type | solution.py:129
  227.9 11.3 %fusion.4 = f32[8,1,16,80]{3,1,2,0:T(1,128)S(1)} fusion(f32[8,128,1,1]{1,2,3,0:T(1,128)S(1)} %bitcast.251, f32[8,128]{1,0:T(8,128)S(1)} %get-tuple-element.41, f32[8,16,80]{2,1,0:T(8,128)S(1)} %broadcast_multiply_fusion.1, f32[8,16]{1,0:T(8,128)S(1)} %get-tuple-element.18, f32[8,16,80,128]{3,2,1,0:T(8,128)S(1)} %bitcast.229), kind=kOutput, calls=%fused_computation.9 | convolution fusion | flops 19660800 | bytes 5333504 | tf_op jit(solution)/shard_map/rhpn,rn->rhp/dot_general | solution.py:136
  240.4 9.8 %psum.14 = f32[8]{0:T(128)S(1)} all-reduce(f32[8]{0:T(128)S(1)} %get-tuple-element.16), channel_id=1, replica_groups=mesh['groups'=2,'seq'=4,'heads'=4] {'heads'}, use_global_device_ids=true, to_apply=%region_5.6 | all-reduce | flops 8 | bytes 64 | tf_op jit(solution)/shard_map/psum | solution.py:142
  250.3 5.3 %all_gather.17 = bf16[32,1280]{1,0:T(8,128)(2,1)S(1)} all-gather(bf16[8,1280]{1,0:T(8,128)(2,1)S(1)} %multiply_convert_fusion.1), channel_id=1, replica_groups=mesh['groups'=2,'seq'=4,'heads'=4] {'seq'}, dimensions={0}, use_global_device_ids=true | all-gather | bytes 102400 | tf_op jit(solution)/shard_map/all_gather | solution.py:148
  258.9 6.8 %copy.120 = bf16[160,8,2,1280]{3,1,2,0:T(8,128)(2,1)} copy(bf16[160,8,2,1280]{3,2,1,0:T(2,128)(2,1)} %bitcast.233) | data formatting | bytes 13107200
  265.8 9.8 %reduce-scatter.3.cloned.1.call-done = f32[8,1280]{1,0:T(8,128)} async-done(((f32[32,1280]{1,0:T(8,128)}), f32[8,1280]{1,0:T(8,128)}) %reduce-scatter.3.cloned.1.call-update) | async-done | bytes 40976 | tf_op jit(solution)/shard_map/reduce_scatter | solution.py:150
  276.4 13.2 %all_gather.18 = bf16[32,1280]{1,0:T(8,128)(2,1)S(1)} all-gather(bf16[8,1280]{1,0:T(8,128)(2,1)S(1)} %add_convert_fusion.3), channel_id=1, replica_groups=mesh['groups'=2,'seq'=4,'heads'=4] {'heads'}, dimensions={0}, use_global_device_ids=true | all-gather | bytes 102400 | tf_op jit(solution)/shard_map/all_gather | solution.py:161
  299.3 5.7 %copy.121 = f32[16,8,80,128]{3,2,1,0:T(8,128)} copy(f32[16,8,80,128]{3,1,2,0:T(8,128)} %bitcast.238) | data formatting | bytes 10485760
  305.0 20.4 %all-reduce.7.cloned.1.call-done = f32[32,2832]{1,0:T(8,128)} async-done(((f32[32,2832]{1,0:T(8,128)}), f32[32,2832]{1,0:T(8,128)}) %all-reduce.7.cloned.1.call-update) | async-done | bytes 362512
  328.2 12.7 %fusion.1 = f32[8,1,16,80]{3,1,2,0:T(1,128)S(1)} fusion(f32[8,128,1,1]{1,2,3,0:T(1,128)S(1)} %bitcast.252, f32[8,128]{1,0:T(8,128)S(1)} %get-tuple-element.31, f32[8,16,80]{2,1,0:T(8,128)S(1)} %broadcast_multiply_fusion, f32[8,16]{1,0:T(8,128)S(1)} %get-tuple-element.14, f32[8,16,80,128]{3,2,1,0:T(8,128)} %bitcast.231), kind=kOutput, calls=%fused_computation.6 | convolution fusion | flops 19660800 | bytes 5333504 | tf_op jit(solution)/shard_map/rhpn,rn->rhp/dot_general | solution.py:136
  341.9 11.7 %psum.15 = f32[8]{0:T(128)S(1)} all-reduce(f32[8]{0:T(128)S(1)} %get-tuple-element.12), channel_id=1, replica_groups=mesh['groups'=2,'seq'=4,'heads'=4] {'heads'}, use_global_device_ids=true, to_apply=%region_9.10 | all-reduce | flops 8 | bytes 64 | tf_op jit(solution)/shard_map/psum | solution.py:142
  353.7 5.3 %all_gather.19 = bf16[32,1280]{1,0:T(8,128)(2,1)S(1)} all-gather(bf16[8,1280]{1,0:T(8,128)(2,1)S(1)} %multiply_convert_fusion), channel_id=1, replica_groups=mesh['groups'=2,'seq'=4,'heads'=4] {'seq'}, dimensions={0}, use_global_device_ids=true | all-gather | bytes 102400 | tf_op jit(solution)/shard_map/all_gather | solution.py:148
  369.2 10.1 %reduce-scatter.5.cloned.1.call-done = f32[8,1280]{1,0:T(8,128)} async-done(((f32[32,1280]{1,0:T(8,128)}), f32[8,1280]{1,0:T(8,128)}) %reduce-scatter.5.cloned.1.call-update) | async-done | bytes 40976 | tf_op jit(solution)/shard_map/reduce_scatter | solution.py:150
  (125 shorter events, 83.3 us)
Async XLA Ops:
  26.4 19.4 %all-to-all-start.6 = ((bf16[4,2,1536]{2,1,0:T(2,128)(2,1)}), bf16[4,2,1536]{2,1,0:T(2,128)(2,1)S(1)}, u32[]{:S(2)}, u32[]{:S(2)}) async-start(bf16[4,2,1536]{2,1,0:T(2,128)(2,1)} %reshape.373), calls=%async_computation.6 | async-start | bytes 49152 | tf_op jit(solution)/shard_map/all_to_all | solution.py:86
  45.8 7.5 %all-to-all-start = ((bf16[4,2,5120]{2,1,0:T(2,128)(2,1)}), bf16[4,2,5120]{2,1,0:T(2,128)(2,1)S(1)}, u32[]{:S(2)}, u32[]{:S(2)}) async-start(bf16[4,2,5120]{2,1,0:T(2,128)(2,1)} %reshape.375), calls=%async_computation | async-start | bytes 163840 | tf_op jit(solution)/shard_map/all_to_all | solution.py:87
  53.3 11.9 %all-to-all-start.4 = ((bf16[2,1,1,3,64,80]{5,0,3,2,1,4:T(2,128)(2,1)}), bf16[2,1,1,3,64,80]{5,0,3,2,1,4:T(2,128)(2,1)S(1)}, u32[]{:S(2)}, u32[]{:S(2)}) async-start(bf16[2,1,1,3,64,80]{5,0,3,2,1,4:T(2,128)(2,1)} %copy.92), calls=%async_computation.4 | async-start | bytes 196608 | tf_op jit(solution)/shard_map/all_to_all | solution.py:79
  65.2 63.7 %all-to-all-start.2 = ((bf16[2,1,1,1,64,10240]{5,0,3,2,1,4:T(2,128)(2,1)}), bf16[2,1,1,1,64,10240]{5,0,3,2,1,4:T(2,128)(2,1)S(1)}, u32[]{:S(2)}, u32[]{:S(2)}) async-start(bf16[2,1,1,1,64,10240]{5,0,3,2,1,4:T(2,128)(2,1)} %copy.109), calls=%async_computation.2 | async-start | bytes 5242880 | tf_op jit(solution)/shard_map/all_to_all | solution.py:78
  81.8 4.0 %copy-start.10 = (u32[32]{0:T(128)S(1)}, u32[32]{0:T(128)}, u32[]{:S(2)}) copy-start(u32[32]{0:T(128)} %constant.94) | copy-start | bytes 388
  128.9 3.3 copy-start.1
  128.9 10.0 %all-to-all-start.1 = ((bf16[8,4,1280]{2,0,1:T(8,128)(2,1)}), bf16[8,4,1280]{2,0,1:T(8,128)(2,1)S(1)}, u32[]{:S(2)}, u32[]{:S(2)}) async-start(bf16[8,4,1280]{2,0,1:T(8,128)(2,1)} %bitcast.76), calls=%async_computation.1 | async-start | bytes 163840 | tf_op jit(solution)/shard_map/all_to_all | solution.py:98
  138.9 8.9 %all-to-all-start.5 = ((bf16[2,8,3,1280]{3,0,2,1:T(2,128)(2,1)}), bf16[2,8,3,1280]{3,0,2,1:T(2,128)(2,1)S(1)}, u32[]{:S(2)}, u32[]{:S(2)}) async-start(bf16[2,8,3,1280]{3,0,2,1:T(2,128)(2,1)} %fusion.26), calls=%async_computation.5 | async-start | bytes 245760 | tf_op jit(solution)/shard_map/all_to_all | solution.py:85
  147.7 5.5 %copy-start.5 = (f32[2,1280]{1,0:T(2,128)S(1)}, f32[2,1280]{1,0:T(2,128)}, u32[]{:S(2)}) copy-start(f32[2,1280]{1,0:T(2,128)} %param.28) | copy-start | bytes 30724
  147.7 5.5 %copy-start.4 = (f32[2,4,1280]{2,1,0:T(4,128)S(1)}, f32[2,4,1280]{2,1,0:T(4,128)}, u32[]{:S(2)}) copy-start(f32[2,4,1280]{2,1,0:T(4,128)} %param.23) | copy-start | bytes 122884
  147.7 5.7 %copy-start.7 = (f32[2,16]{1,0:T(2,128)S(1)}, f32[2,16]{1,0:T(2,128)}, u32[]{:S(2)}) copy-start(f32[2,16]{1,0:T(2,128)} %param.27) | copy-start | bytes 388
  147.7 5.7 %copy-start.8 = (f32[2,16]{1,0:T(2,128)S(1)}, f32[2,16]{1,0:T(2,128)}, u32[]{:S(2)}) copy-start(f32[2,16]{1,0:T(2,128)} %param.25) | copy-start | bytes 388
  147.7 5.7 %copy-start.9 = (f32[2,16]{1,0:T(2,128)S(1)}, f32[2,16]{1,0:T(2,128)}, u32[]{:S(2)}) copy-start(f32[2,16]{1,0:T(2,128)} %param.26) | copy-start | bytes 388
  147.7 5.7 %copy-start.6 = (f32[2,4,256]{2,1,0:T(4,128)S(1)}, f32[2,4,256]{2,1,0:T(4,128)}, u32[]{:S(2)}) copy-start(f32[2,4,256]{2,1,0:T(4,128)} %param.24) | copy-start | bytes 24580
  147.7 6.0 %copy-start.3 = (bf16[2,1280,16]{1,2,0:T(8,128)(2,1)S(1)}, bf16[2,1280,16]{1,2,0:T(8,128)(2,1)}, u32[]{:S(2)}) copy-start(bf16[2,1280,16]{1,2,0:T(8,128)(2,1)} %param.21) | copy-start | bytes 245764
  147.7 6.1 %copy-start.2 = (bf16[2,1280,256]{2,1,0:T(8,128)(2,1)S(1)}, bf16[2,1280,256]{2,1,0:T(8,128)(2,1)}, u32[]{:S(2)}) copy-start(bf16[2,1280,256]{2,1,0:T(8,128)(2,1)} %param.22) | copy-start | bytes 3932164
  147.8 70.9 %all-to-all-start.3 = ((bf16[2,8,16,10240]{3,2,0,1:T(8,128)(2,1)}), bf16[2,8,16,10240]{3,2,0,1:T(8,128)(2,1)}, u32[]{:S(2)}, u32[]{:S(2)}) async-start(bf16[2,8,16,10240]{3,2,0,1:T(8,128)(2,1)} %select_bitcast_fusion), calls=%async_computation.3 | async-start | bytes 10485760 | tf_op jit(solution)/shard_map/all_to_all | solution.py:84
  153.0 40.1 %all-reduce.5.cloned.1.call-start = ((), (), s32[]{:S(2)}) async-start(), calls=%async_computation.11 | async-start | bytes 753664
  159.0 116.6 %reduce-scatter.3.cloned.1.call-start = ((), (), s32[]{:S(2)}) async-start(), calls=%async_computation.9 | async-start | bytes 204800 | tf_op jit(solution)/shard_map/reduce_scatter | solution.py:150
  225.7 2.3 copy-start
  258.8 66.6 %all-reduce.7.cloned.1.call-start = ((), (), s32[]{:S(2)}) async-start(), calls=%async_computation.12 | async-start | bytes 753664
  294.9 84.4 %reduce-scatter.5.cloned.1.call-start = ((), (), s32[]{:S(2)}) async-start(), calls=%async_computation.10 | async-start | bytes 204800 | tf_op jit(solution)/shard_map/reduce_scatter | solution.py:150
Sparse Core Ops, SparseCore 0:
  159.1 33.9 all-reduce.4
  259.0 16.5 reduce-scatter.2
  295.0 30.3 all-reduce.6
  362.4 16.8 reduce-scatter.4
where the time goes:
time: 389 us; the launch traced here: 387 us
  waiting for transfers between devices  139 us (36%)
  blocking collectives  73.6 us (19%)
  local copies, waits for them, and re-layouts  54.5 us (14%)
  matrix products  39.4 us (10%)
  other arithmetic  36.9 us (9%)
  starting transfers between devices  28.6 us (7%)
  between operations  14.9 us (4%)
    unnamed x6, waiting for transfers between devices  54.3 us
    all_to_all x1, waiting for transfers between devices, on_device(): lax.all_to_all(state_send, 'heads', split_axis=4, concat_axis=1, tiled=True)  39.7 us
    dot_general x2, matrix products, on_device(): jnp.einsum('rhpn,rn->rhp', fresh_state, output_matrix, precision=lax.Prec...  24 us
    all_to_all x1, waiting for transfers between devices, on_device(): lax.all_to_all(select_rows(state_heads, 1), 'seq', split_axis=1, concat_a...  22.9 us
    unnamed x36, local copies, waits for them, and re-layouts  22.2 us
    psum x2, blocking collectives, on_device(): sum_sq = lax.psum(jnp.sum(gated * gated, axis=1), 'heads')  21.5 us
    reduce_scatter x2, waiting for transfers between devices, on_device(): lax.psum_scatter(jnp.dot(mixed_all, weight_out, preferred_element_type=jn...  19.9 us
    all_gather x1, blocking collectives, on_device(): lax.all_gather(matrix_tail, 'heads', axis=0, tiled=True)  14.8 us
  transfers between devices with their start and end apart: 11, of which 7 were waited for; matrix products, arithmetic and copies ran while one was open for 19% of the time, Pallas kernels for 0%

commit v1 on v0

v1 whole, which is shorter than its diff:
```python
import functools

import jax
import jax.numpy as jnp
from jax import lax
from jax.experimental import pallas as pl
from jax.experimental.pallas import tpu as pltpu
from jax.sharding import PartitionSpec as P

epsilon = 1e-05
f32 = jnp.float32
bf16 = jnp.bfloat16
MESH = pl.DeviceIdType.MESH


def silu(v):
    return v / (1.0 + jnp.exp(-v))


def kernel(
    dims,
    select_ref,
    state_hbm,
    tails_ref,
    mtails_ref,
    hidden_ref,
    rows_ref,
    win_hbm,
    wstep_hbm,
    wmat_hbm,
    cconv_ref,
    mconv_ref,
    sbias_ref,
    dlog_ref,
    skip_ref,
    ngain_ref,
    wout_hbm,
    decoded_ref,
    newstate_hbm,
    win,
    wout,
    wstep,
    wmat,
    outbox,
    hid_in,
    tails_in,
    mtails_in,
    rows_in,
    tails_rows,
    mtails_rows,
    current,
    spread,
    zx,
    zx_send,
    zx_recv,
    sm_send,
    sm_recv,
    flip_a,
    flip_b,
    col_a,
    col_b,
    col_y,
    gated_all,
    gated_send,
    ss_all,
    normed_ref,
    part,
    part_recv,
    result_send,
    local_sem,
    state_ssem,
    state_rsem,
    tok_ssem,
    tok_rsem,
    row_ssem,
    row_rsem,
    tail_ssem,
    tail_rsem,
    mt_ssem,
    mt_rsem,
    zx_ssem,
    zx_rsem,
    sm_ssem,
    sm_rsem,
    g_ssem,
    g_rsem,
    ss_ssem,
    ss_rsem,
    part_ssem,
    part_rsem,
    res_ssem,
    res_rsem,
    out_ssem,
    out_rsem,
    *state,
):
    layers, heads_n, seq_n, members, head_dev, head_width, width, channels, pair, taps = dims
    requests = seq_n * members
    chunk_rows = requests // heads_n
    share_rows = decoded_ref.shape[0]
    model_width = width * seq_n
    s_me = lax.axis_index("seq")
    h_me = lax.axis_index("heads")
    me = s_me * heads_n + h_me
    devices = seq_n * heads_n
    channels_pad = flip_a.shape[1]

    loads = []

    def load(src, dst, index):
        copy = pltpu.make_async_copy(src, dst, local_sem.at[index])
        copy.start()
        return copy

    def peer(offset):
        other = lax.rem(me + offset, devices)
        return other // heads_n, lax.rem(other, heads_n)

    win_load = [load(win_hbm.at[l], win.at[l], l) for l in range(layers)]
    wout_load = [load(wout_hbm.at[l], wout.at[l], layers + l) for l in range(layers)]
    wstep_load = load(wstep_hbm, wstep, 2 * layers)
    wmat_load = load(wmat_hbm, wmat, 2 * layers + 1)
    own_load = [
        load(
            state_hbm.at[l, 0, 0, pl.ds(h_me * head_dev, head_dev)],
            state[l].at[h_me],
            2 * layers + 2 + l,
        )
        for l in range(layers)
    ]

    barrier = pltpu.get_barrier_semaphore()

    @pl.loop(1, devices)
    def _(offset):
        s_to, h_to = peer(offset)
        pl.semaphore_signal(
            barrier, inc=1, device_id={"seq": s_to, "heads": h_to}, device_id_type=MESH
        )

    pl.semaphore_wait(barrier, devices - 1)

    pending = []

    def remote(src, dst, ssem, rsem, where):
        copy = pltpu.make_async_remote_copy(
            src_ref=src,
            dst_ref=dst,
            send_sem=ssem,
            recv_sem=rsem,
            device_id=where,
            device_id_type=MESH,
        )
        copy.start()
        pending.append(copy)
        return copy

    def token_copy(offset):
        s_to, h_to = peer(offset)
        return pltpu.make_async_remote_copy(
            src_ref=hidden_ref.at[s_to],
            dst_ref=hid_in.at[me],
            send_sem=tok_ssem.at[offset],
            recv_sem=tok_rsem.at[offset],
            device_id={"seq": s_to, "heads": h_to},
            device_id_type=MESH,
        )

    @pl.loop(1, devices)
    def _(offset):
        token_copy(offset).start()

    row_copies = [
        remote(
            rows_ref,
            rows_in.at[s_me],
            row_ssem.at[d],
            row_rsem.at[d],
            {"seq": lax.rem(s_me + d, seq_n)},
        )
        for d in range(1, seq_n)
    ]
    tail_copies = []
    for d in range(1, heads_n):
        h_to = lax.rem(h_me + d, heads_n)
        tail_copies.append(
            remote(
                tails_ref.at[h_to],
                tails_in.at[h_me],
                tail_ssem.at[d],
                tail_rsem.at[d],
                {"heads": h_to},
            )
        )
        tail_copies.append(
            remote(
                mtails_ref, mtails_in.at[h_me], mt_ssem.at[d], mt_rsem.at[d], {"heads": h_to}
            )
        )

    def send_state(l):
        copies = []
        for d in range(1, heads_n):
            h_to = lax.rem(h_me + d, heads_n)
            copies.append(
                remote(
                    state_hbm.at[l, 0, 0, pl.ds(h_to * head_dev, head_dev)],
                    state[l].at[h_me],
                    state_ssem.at[l, d],
                    state_rsem.at[l, d],
                    {"heads": h_to},
                )
            )
        return copies

    state_copies = {0: send_state(0)}

    hid_in[me] = hidden_ref[s_me]
    rows_in[s_me] = rows_ref[...]
    tails_in[h_me] = tails_ref[h_me]
    mtails_in[h_me] = mtails_ref[...]

    @pl.loop(1, devices)
    def _(offset):
        token_copy(offset).wait_recv()

    for r in range(requests):
        current[r // chunk_rows, r % chunk_rows : r % chunk_rows + 1, :] = hid_in[r]

    even = lax.broadcasted_iota(jnp.int32, (128, 256), 1) - 2 * lax.broadcasted_iota(
        jnp.int32, (128, 256), 0
    )
    pick = [(even == 0).astype(bf16), (even == 1).astype(bf16)]
    expand = lax.broadcasted_iota(jnp.int32, (head_dev, channels), 1) - head_width * (
        lax.broadcasted_iota(jnp.int32, (head_dev, channels), 0)
    )
    expand = ((expand >= 0) & (expand < head_width)).astype(f32)

    def per_channel(values):
        return jnp.dot(
            values, expand, precision=lax.Precision.HIGHEST, preferred_element_type=f32
        )

    block = 256 if channels % 256 == 0 else channels
    block_out = 256 if width % 256 == 0 else width
    group_heads = 4 if head_dev % 4 == 0 else head_dev
    group_rows = group_heads * head_width

    for l in range(layers):
        hidden = jnp.concatenate([current[c] for c in range(heads_n)], axis=0).astype(bf16)
        for k in range(width // 128):
            part_h = hidden[:, k * 128 : (k + 1) * 128]
            for half in range(2):
                spread[half * requests : (half + 1) * requests, k * 256 : (k + 1) * 256] = jnp.dot(
                    part_h, pick[half], preferred_element_type=f32
                ).astype(bf16)
        win_load[l].wait()
        weight = win.at[l].reshape(2 * width, channels)
        if block == channels:
            zx[...] = jnp.dot(spread[...], weight[...], preferred_element_type=f32)
        else:

            @pl.loop(0, channels // block)
            def _(n):
                cols = pl.ds(pl.multiple_of(n * block, block), block)
                zx[:, cols] = jnp.dot(spread[...], weight[:, cols], preferred_element_type=f32)

        if l == 0:
            wstep_load.wait()
            wmat_load.wait()
        step_part = jnp.dot(hidden, wstep[l], preferred_element_type=f32)
        mat_part = jnp.dot(hidden, wmat[l], preferred_element_type=f32)
        for q in range(seq_n):
            rows = slice(q * members, (q + 1) * members)
            zx_send[l, q, 0] = zx[q * members : (q + 1) * members, :]
            zx_send[l, q, 1] = zx[requests + q * members : requests + (q + 1) * members, :]
            sm_send[l, q, :, 0:256] = mat_part[rows]
            sm_send[l, q, :, 256 : 256 + head_dev] = step_part[rows]
        copies = []
        for d in range(1, seq_n):
            s_to = lax.rem(s_me + d, seq_n)
            copies.append(
                remote(
                    zx_send.at[l, s_to],
                    zx_recv.at[l, d],
                    zx_ssem.at[l, d],
                    zx_rsem.at[l, d],
                    {"seq": s_to},
                )
            )
            copies.append(
                remote(
                    sm_send.at[l, s_to],
                    sm_recv.at[l, d],
                    sm_ssem.at[l, d],
                    sm_rsem.at[l, d],
                    {"seq": s_to},
                )
            )
        if l == 0:
            for copy in tail_copies + row_copies:
                copy.wait_recv()
            for m in range(members):
                for i in range(layers * (taps - 1)):
                    tails_rows[i, m : m + 1, :] = tails_in[m, i : i + 1, :]
                    mtails_rows[i, m : m + 1, :] = mtails_in[m, i : i + 1, :]
        for copy in copies:
            copy.wait_recv()
        zx_sum = zx_send[l, s_me]
        sm_sum = sm_send[l, s_me]
        for d in range(1, seq_n):
            zx_sum = zx_sum + zx_recv[l, d]
            sm_sum = sm_sum + sm_recv[l, d]
        gate = zx_sum[0]
        conv_x = cconv_ref[l, taps - 1 : taps, :] * zx_sum[1]
        conv_m = mconv_ref[l, taps - 1 : taps, :] * sm_sum[:, 0:256]
        for j in range(taps - 1):
            conv_x = conv_x + cconv_ref[l, j : j + 1, :] * tails_rows[l * (taps - 1) + j]
            conv_m = conv_m + mconv_ref[l, j : j + 1, :] * mtails_rows[l * (taps - 1) + j]
        conv_x = silu(conv_x)
        conv_m = silu(conv_m)
        half_m = conv_m.shape[1] // 2
        step_in = sm_sum[:, 256 : 256 + head_dev] + sbias_ref[l : l + 1, :]
        step = jnp.maximum(step_in, 0.0) + jnp.log1p(jnp.exp(-jnp.abs(step_in)))
        decay = jnp.exp(-jnp.exp(dlog_ref[l : l + 1, :]) * step)
        flip_a[0:members, 0:channels] = per_channel(decay)
        flip_b[0:members, 0:channels] = per_channel(step) * conv_x
        skip = per_channel(jnp.broadcast_to(skip_ref[l : l + 1, :], (8, head_dev)))[0:1]
        for k in range(channels_pad // 128):
            cols = slice(k * 128, (k + 1) * 128)
            col_a[cols, :] = flip_a[:, cols].T
            col_b[cols, :] = flip_b[:, cols].T

        own_load[l].wait()
        for copy in state_copies[l]:
            copy.wait_recv()
        if l + 1 < layers:
            state_copies[l + 1] = send_state(l + 1)

        lane = lax.broadcasted_iota(jnp.int32, (group_rows, 128), 1)

        @pl.loop(0, head_dev // group_heads)
        def _(i):
            rows = pl.ds(pl.multiple_of(i * group_rows, 8), group_rows)
            heads = pl.ds(i * group_heads, group_heads)
            total = jnp.zeros((group_rows, 128), f32)
            for m in range(members):
                old = state[l][m, heads].reshape(group_rows, half_m).astype(f32)
                fresh = (
                    col_a[rows, m : m + 1] * old
                    + col_b[rows, m : m + 1] * conv_m[m : m + 1, 0:half_m]
                )
                read = jnp.sum(fresh * conv_m[m : m + 1, half_m:], axis=1, keepdims=True)
                total = jnp.where(lane == m, read, total)
                state[l][m, heads] = fresh.astype(bf16).reshape(group_heads, head_width, half_m)
            col_y[rows, :] = total

        for k in range(channels_pad // 128):
            cols = slice(k * 128, (k + 1) * 128)
            flip_a[:, cols] = col_y[cols, :].T
        gated = (flip_a[0:members, 0:channels] + skip * conv_x) * silu(gate)
        gated_send[l] = gated
        gated_all[l, s_me] = gated
        square = jnp.broadcast_to(jnp.sum(gated * gated, axis=1, keepdims=True), (members, 128))
        ss_all[l, me] = square
        g_copies = []
        for d in range(1, seq_n):
            g_copies.append(
                remote(
                    gated_send.at[l],
                    gated_all.at[l, s_me],
                    g_ssem.at[l, d],
                    g_rsem.at[l, d],
                    {"seq": lax.rem(s_me + d, seq_n)},
                )
            )

        def square_copy(offset):
            s_to, h_to = peer(offset)
            return pltpu.make_async_remote_copy(
                src_ref=ss_all.at[l, me],
                dst_ref=ss_all.at[l, me],
                send_sem=ss_ssem.at[l, offset],
                recv_sem=ss_rsem.at[l, offset],
                device_id={"seq": s_to, "heads": h_to},
                device_id_type=MESH,
            )

        @pl.loop(1, devices)
        def _(offset):
            square_copy(offset).start()

        def send_rows():
            @pl.loop(0, seq_n * pair)
            def _(slot):
                source = select_ref[0, slot]
                keep = select_ref[1, slot].astype(f32).astype(bf16)
                q_to = slot // pair
                k_to = lax.rem(slot, pair)

                @pl.loop(0, head_dev // group_heads)
                def _(i):
                    heads = pl.ds(i * group_heads, group_heads)
                    outbox[l, q_to, k_to, heads] = state[l][source, heads] * keep

            for d in range(1, seq_n):
                s_to = lax.rem(s_me + d, seq_n)
                remote(
                    outbox.at[l, s_to],
                    newstate_hbm.at[l, 0, pl.ds(s_me * pair, pair)],
                    out_ssem.at[l, d],
                    out_rsem.at[l, d],
                    {"seq": s_to},
                )
            own = pltpu.make_async_copy(
                outbox.at[l, s_me],
                newstate_hbm.at[l, 0, pl.ds(s_me * pair, pair)],
                local_sem.at[3 * layers + 2 + l],
            )
            own.start()
            loads.append(own)

        send_rows()

        for copy in g_copies:
            copy.wait_recv()

        @pl.loop(1, devices)
        def _(offset):
            square_copy(offset).wait()

        for q in range(seq_n):
            total_sq = ss_all[l, q * heads_n]
            for h in range(1, heads_n):
                total_sq = total_sq + ss_all[l, q * heads_n + h]
            scale = lax.rsqrt(total_sq[:, 0:1] / model_width + epsilon)
            normed_ref[q * members : (q + 1) * members, :] = (
                gated_all[l, q] * scale * ngain_ref[l : l + 1, :]
            )
        wout_load[l].wait()
        normed = normed_ref[...].astype(bf16)
        if block_out == width:
            zout = jnp.dot(normed, wout[l], preferred_element_type=f32)
            for c in range(heads_n):
                part[l, c] = zout[c * chunk_rows : (c + 1) * chunk_rows]
        else:

            @pl.loop(0, width // block_out)
            def _(n):
                cols = pl.ds(pl.multiple_of(n * block_out, block_out), block_out)
                zout = jnp.dot(normed, wout[l, :, cols], preferred_element_type=f32)
                for c in range(heads_n):
                    part[l, c, :, cols] = zout[c * chunk_rows : (c + 1) * chunk_rows]

        copies = []
        for d in range(1, heads_n):
            h_to = lax.rem(h_me + d, heads_n)
            copies.append(
                remote(
                    part.at[l, h_to],
                    part_recv.at[l, d],
                    part_ssem.at[l, d],
                    part_rsem.at[l, d],
                    {"heads": h_to},
                )
            )
        for copy in copies:
            copy.wait_recv()
        summed = part[l, h_me]
        for d in range(1, heads_n):
            summed = summed + part_recv[l, d]
        base = current if l == 0 else result_send.at[l - 1]
        result_send[l, h_me] = (base[h_me] + summed).astype(bf16).astype(f32)
        copies = []
        for d in range(1, heads_n):
            h_to = lax.rem(h_me + d, heads_n)
            copies.append(
                remote(
                    result_send.at[l, h_me],
                    result_send.at[l, h_me],
                    res_ssem.at[l, d],
                    res_rsem.at[l, d],
                    {"heads": h_to},
                )
            )
        for copy in copies:
            copy.wait_recv()
        current_next = result_send.at[l]
        if l + 1 < layers:
            for c in range(heads_n):
                current[c] = current_next[c]
            if l == 0:
                pass

    final = jnp.concatenate([result_send[layers - 1, c] for c in range(heads_n)], axis=0)
    targets = jnp.concatenate([rows_in[q] for q in range(seq_n)], axis=0)
    wanted = (h_me * share_rows).astype(f32) + lax.broadcasted_iota(
        jnp.int32, (requests, 128), 1
    ).astype(f32)
    hot = (targets == wanted).astype(f32).astype(bf16)
    chosen = lax.dot_general(
        hot, final.astype(bf16), (((0,), (0,)), ((), ())), preferred_element_type=f32
    )
    decoded_ref[...] = chosen[0:share_rows].astype(bf16)

    @pl.loop(1, devices)
    def _(offset):
        token_copy(offset).wait_send()

    for copy in loads:
        copy.wait()
    for copy in pending:
        copy.wait_send()
    for l in range(layers):
        for d in range(1, seq_n):
            pltpu.make_async_remote_copy(
                src_ref=outbox.at[l, s_me],
                dst_ref=newstate_hbm.at[
                    l, 0, pl.ds(lax.rem(s_me + seq_n - d, seq_n) * pair, pair)
                ],
                send_sem=out_ssem.at[l, d],
                recv_sem=out_rsem.at[l, d],
                device_id={"seq": lax.rem(s_me + d, seq_n)},
                device_id_type=MESH,
            ).wait_recv()


def on_device(
    final_state,
    channel_tail,
    matrix_tail,
    last_hidden,
    decode_group,
    input_weight,
    step_weight,
    matrix_weight,
    channel_conv,
    matrix_conv,
    step_bias,
    decay_log,
    skip_gain,
    norm_gain,
    output_weight,
):
    heads_n = lax.axis_size("heads")
    seq_n = lax.axis_size("seq")
    layers, _, slots, heads_all, head_width, state_width = final_state.shape
    head_dev = heads_all // heads_n
    model_width = last_hidden.shape[2]
    width = model_width // seq_n
    taps = channel_conv.shape[1]
    members = heads_n * slots
    pair = 2 * members // seq_n
    capacity = seq_n * pair
    requests = seq_n * members
    share_rows = capacity * seq_n // heads_n
    chunk_rows = requests // heads_n
    channels = head_dev * head_width
    channels_pad = -(-channels // 128) * 128
    tail_rows = layers * (taps - 1)
    devices = seq_n * heads_n

    dest = decode_group[:, 0]
    member_ids = jnp.arange(members, dtype=jnp.int32)
    earlier = (dest[:, None] == dest[None, :]) & (member_ids[None, :] < member_ids[:, None])
    rank = jnp.sum(earlier.astype(jnp.int32), axis=1)
    target = dest * pair + rank
    matches = target[None, :] == jnp.arange(capacity, dtype=jnp.int32)[:, None]
    source = jnp.sum(jnp.where(matches, member_ids[None, :], 0), axis=1)
    filled = jnp.sum(matches.astype(jnp.int32), axis=1)
    select = jnp.stack([source, filled])
    row = dest * capacity + lax.axis_index("seq") * pair + rank
    rows = jnp.broadcast_to(row.astype(f32)[:, None], (members, 128))

    tails = jnp.transpose(
        channel_tail.reshape(tail_rows, heads_n, channels), (1, 0, 2)
    ).astype(f32)
    mtails = matrix_tail.reshape(tail_rows, 2 * state_width).astype(f32)
    hidden = last_hidden.reshape(seq_n, 1, width).astype(f32)

    dims = (
        layers, heads_n, seq_n, members, head_dev, head_width, width, channels, pair, taps
    )
    vmem = pl.BlockSpec(memory_space=pltpu.VMEM)
    smem = pl.BlockSpec(memory_space=pltpu.SMEM)
    anyw = pl.BlockSpec(memory_space=pl.ANY)
    V = pltpu.VMEM
    dma = pltpu.SemaphoreType.DMA
    scratch = [
        V((layers, width, 2, channels), bf16),
        V((layers, channels, width), bf16),
        V((layers, width, head_dev), bf16),
        V((layers, width, 2 * state_width), bf16),
        V((layers, seq_n, pair, head_dev, head_width, state_width), bf16),
        V((requests, 1, width), f32),
        V((heads_n, tail_rows, channels), f32),
        V((heads_n, tail_rows, 2 * state_width), f32),
        V((seq_n, members, 128), f32),
        V((tail_rows, members, channels), f32),
        V((tail_rows, members, 2 * state_width), f32),
        V((heads_n, chunk_rows, width), f32),
        V((2 * requests, 2 * width), bf16),
        V((2 * requests, channels), f32),
        V((layers, seq_n, 2, members, channels), f32),
        V((layers, seq_n, 2, members, channels), f32),
        V((layers, seq_n, members, 384), f32),
        V((layers, seq_n, members, 384), f32),
        V((128, channels_pad), f32),
        V((128, channels_pad), f32),
        V((channels_pad, 128), f32),
        V((channels_pad, 128), f32),
        V((channels_pad, 128), f32),
        V((layers, seq_n, members, channels), f32),
        V((layers, members, channels), f32),
        V((layers, devices, members, 128), f32),
        V((requests, channels), f32),
        V((layers, heads_n, chunk_rows, width), f32),
        V((layers, heads_n, chunk_rows, width), f32),
        V((layers, heads_n, chunk_rows, width), f32),
        dma((4 * layers + 2,)),
        dma((layers, heads_n)),
        dma((layers, heads_n)),
        dma((devices,)),
        dma((devices,)),
        dma((seq_n,)),
        dma((seq_n,)),
        dma((heads_n,)),
        dma((heads_n,)),
        dma((heads_n,)),
        dma((heads_n,)),
        dma((layers, seq_n)),
        dma((layers, seq_n)),
        dma((layers, seq_n)),
        dma((layers, seq_n)),
        dma((layers, seq_n)),
        dma((layers, seq_n)),
        dma((layers, devices)),
        dma((layers, devices)),
        dma((layers, heads_n)),
        dma((layers, heads_n)),
        dma((layers, heads_n)),
        dma((layers, heads_n)),
        dma((layers, seq_n)),
        dma((layers, seq_n)),
    ] + [V((members, head_dev, head_width, state_width), bf16) for _ in range(layers)]
    decoded, new_state = pl.pallas_call(
        functools.partial(kernel, dims),
        out_shape=(
            jax.ShapeDtypeStruct((share_rows, width), bf16),
            jax.ShapeDtypeStruct(
                (layers, 1, capacity, head_dev, head_width, state_width), bf16
            ),
        ),
        in_specs=[
            smem, anyw, vmem, vmem, vmem, vmem, anyw, anyw, anyw,
            vmem, vmem, vmem, vmem, vmem, vmem, anyw,
        ],
        out_specs=(vmem, anyw),
        scratch_shapes=scratch,
        compiler_params=pltpu.CompilerParams(
            collective_id=0, has_side_effects=True, vmem_limit_bytes=58 * 1024 * 1024
        ),
        cost_estimate=pl.CostEstimate(
            flops=4 * requests * width * channels * 3 * layers,
            bytes_accessed=30_000_000,
            transcendentals=0,
        ),
        name="handover",
    )(
        select,
        final_state,
        tails,
        mtails,
        hidden,
        rows,
        input_weight,
        step_weight,
        matrix_weight,
        channel_conv,
        matrix_conv,
        step_bias,
        decay_log,
        skip_gain,
        norm_gain,
        output_weight,
    )
    return decoded, new_state


def solution(mesh):
    return jax.shard_map(
        on_device,
        mesh=mesh,
        in_specs=(
            P(None, ("groups", "seq", "heads"), None, None, None, None),
            P(None, ("groups", "seq", "heads"), None, None, None),
            P(("groups", "seq", "heads"), None, None, None, None),
            P(("groups", "seq", "heads"), None, None),
            P(("groups", "seq"), None),
            P(None, "seq", None, "heads"),
            P(None, "seq", "heads"),
            P(None, "seq", None),
            P(None, None, "heads"),
            P(),
            P(None, "heads"),
            P(None, "heads"),
            P(None, "heads"),
            P(None, "heads"),
            P(None, "heads", "seq"),
        ),
        out_specs=(
            P(("groups", "heads"), "seq"),
            P(None, ("groups", "seq"), None, "heads", None, None),
        ),
        check_vma=False,
    )
```

time: 389 us -> 143 us (0.37)
  waiting for transfers between devices: 139 us -> 0 us
  Pallas kernels: 0 us -> 124 us
  blocking collectives: 73.6 us -> 0 us
  local copies, waits for them, and re-layouts: 54.5 us -> 12.9 us
  matrix products: 39.4 us -> 0 us
  other arithmetic: 36.9 us -> 4.22 us
  starting transfers between devices: 28.6 us -> 0 us
  between operations: 14.9 us -> 0.66 us
    pallas_call x0 -> x1, Pallas kernels: none -> 124 us  [on_device(): pl.pallas_call(functools.partial(kernel, dims), out_shape=(jax.ShapeDtype...]
    all_to_all x7 -> x0, waiting for transfers between devices: 65.1 us -> none  [the longest x1 39.7 us: on_device(): lax.all_to_all(state_send, 'heads', split_axis=4, concat_axis=1, tiled=True)]
    unnamed x6 -> x0, waiting for transfers between devices: 54.3 us -> none
    all_gather x5 -> x0, blocking collectives: 52.1 us -> none  [the longest x1 14.8 us: on_device(): lax.all_gather(matrix_tail, 'heads', axis=0, tiled=True)]
    dot_general x10 -> x0, matrix products: 39.4 us -> none  [the longest x2 24 us: on_device(): jnp.einsum('rhpn,rn->rhp', fresh_state, output_matrix, precision=lax.Prec...]
    all_to_all x7 -> x0, starting transfers between devices: 28.1 us -> none  [the longest x1 5.19 us: on_device(): lax.all_to_all(select_rows(state_heads, 1), 'seq', split_axis=1, concat_a...]
    psum x2 -> x0, blocking collectives: 21.5 us -> none  [on_device(): sum_sq = lax.psum(jnp.sum(gated * gated, axis=1), 'heads')]
    reduce_scatter x2 -> x0, waiting for transfers between devices: 19.9 us -> none  [on_device(): lax.psum_scatter(jnp.dot(mixed_all, weight_out, preferred_element_type=jn...]
  transfers between devices with their start and end apart: 11 -> 0, of which waited for: 7 -> 0; matrix products, arithmetic and copies ran while one was open for 19% -> 0% of each run, Pallas kernels for 0% -> 0%
where the time goes in v1:
time: 143 us; the launch traced here: 142 us
  Pallas kernels  124 us (87%)
  local copies, waits for them, and re-layouts  12.9 us (9%)
  other arithmetic  4.22 us (3%)
    pallas_call x1, Pallas kernels, on_device(): pl.pallas_call(functools.partial(kernel, dims), out_shape=(jax.ShapeDtype...  124 us
    unnamed x3, local copies, waits for them, and re-layouts  9.27 us

profile of v1, /device:TPU:0, one launch (start us, length us, event | category | flops | bytes accessed | tf_op | source)
XLA Modules:
  0.0 142.2 jit_solution(3709996260508024565)
XLA Ops:
  0.6 0.9 convert_reduce_fusion.1
  1.5 0.7 fusion.2
  2.2 0.7 multiply_add_fusion
  2.9 0.1 select_reduce_fusion
  3.0 0.5 pad_add_fusion.select_ref
  3.5 0.6 broadcast_in_dim.28.rows_ref
  4.2 0.7 copy.25
  4.8 0.6 reshape.35.mtails_ref
  5.4 1.4 convert.4.hidden_ref
  6.8 0.9 copy.23
  7.7 0.1 reshape.37
  7.8 0.7 copy.28
  8.5 2.0 %copy.26.wstep_hbm = bf16[2,1280,16]{2,1,0:T(8,128)(2,1)} copy(bf16[2,1280,16]{1,2,0:T(8,128)(2,1)} %param.21) | data formatting | bytes 163840 | tf_op args[6]
  10.4 124.5 %handover.1 = (bf16[8,1280]{1,0:T(8,128)(2,1)}, bf16[2,1,8,16,80,128]{5,4,3,2,1,0:T(8,128)(2,1)}) custom-call(s32[2,8]{1,0:T(2,128)} %pad_add_fusion.select_ref, bf16[2,1,1,64,80,128]{5,4,3,2,1,0:T(8,128)(2,1)} %state_hbm.1, f32[4,6,1280]{2,1,0:T(8,128)} %bitcast.19, f32[6,256]{1,0:T(8,128)} %reshape.35.mtails_ref, f32[4,1,1280]{2,1,0:T(1,128)} %convert.4.hidden_ref, ...), custom_call_target="tpu_custom_call" | custom-call | flops 629145600 | bytes 30000000 | tf_op jit(solution)/shard_map/handover/pallas_call | solution.py:646
  134.9 1.3 copy.31
  136.2 6.0 %copy.32 = bf16[2,1,8,16,80,128]{5,4,3,2,1,0:T(8,128)(2,1)} copy(bf16[2,1,8,16,80,128]{5,4,3,2,1,0:T(8,128)(2,1)} %get-tuple-element.7) | data formatting | bytes 10485760

commit v2 on v1

--- a/solution.py
+++ b/solution.py
@@ -19,12 +19,11 @@
 
 def kernel(
     dims,
-    select_ref,
+    group_ref,
     state_hbm,
-    tails_ref,
-    mtails_ref,
-    hidden_ref,
-    rows_ref,
+    tails_arg,
+    mtails_arg,
+    hidden_arg,
     win_hbm,
     wstep_hbm,
     wmat_hbm,
@@ -36,7 +35,8 @@
     ngain_ref,
     wout_hbm,
     decoded_ref,
-    newstate_hbm,
+    raw_hbm,
+    vec_hbm,
     win,
     wout,
     wstep,
@@ -56,10 +56,13 @@
     sm_send,
     sm_recv,
     flip_a,
-    flip_b,
-    col_a,
-    col_b,
     col_y,
+    tails_ref,
+    mtails_ref,
+    hidden_ref,
+    rows_ref,
+    vec_rows,
+    vec_send,
     gated_all,
     gated_send,
     ss_all,
@@ -92,7 +95,9 @@
     res_rsem,
     out_ssem,
     out_rsem,
-    *state,
+    vec_ssem,
+    vec_rsem,
+    *state_flat,
 ):
     layers, heads_n, seq_n, members, head_dev, head_width, width, channels, pair, taps = dims
     requests = seq_n * members
@@ -104,6 +109,12 @@
     me = s_me * heads_n + h_me
     devices = seq_n * heads_n
     channels_pad = flip_a.shape[1]
+    group_heads = 4 if head_dev % 4 == 0 else head_dev
+    group_rows = group_heads * head_width
+    chunks = head_dev // group_heads
+    steps = [(l, c) for l in range(layers) for c in range(chunks)]
+    state = [[state_flat[l * chunks + c] for c in range(chunks)] for l in range(layers)]
+    capacity = seq_n * pair
 
     loads = []
 
@@ -122,12 +133,43 @@
     wmat_load = load(wmat_hbm, wmat, 2 * layers + 1)
     own_load = [
         load(
-            state_hbm.at[l, 0, 0, pl.ds(h_me * head_dev, head_dev)],
-            state[l].at[h_me],
-            2 * layers + 2 + l,
-        )
-        for l in range(layers)
+            state_hbm.at[l, 0, 0, pl.ds(h_me * head_dev + c * group_heads, group_heads)],
+            state[l][c].at[h_me],
+            2 * layers + 2 + l * chunks + c,
+        )
+        for l, c in steps
     ]
+
+    for j in range(taps - 1):
+        chan = tails_arg[j].astype(f32)
+        matr = mtails_arg[j].astype(f32)
+        for l in range(layers):
+            i = l * (taps - 1) + j
+            mtails_ref[i : i + 1, :] = matr[l : l + 1]
+            for h in range(heads_n):
+                tails_ref[h, i : i + 1, :] = chan[l : l + 1, h * channels : (h + 1) * channels]
+    for q in range(seq_n):
+        hidden_ref[q] = hidden_arg[q].astype(f32)
+    dest = [group_ref[m] for m in range(members)]
+    one, zero = jnp.int32(1), jnp.int32(0)
+    rank = []
+    for m in range(members):
+        count = zero
+        for e in range(m):
+            count = count + jnp.where(dest[e] == dest[m], one, zero)
+        rank.append(count)
+    for m in range(members):
+        row = dest[m] * capacity + s_me * pair + rank[m]
+        rows_ref[m : m + 1, :] = jnp.full((1, 128), row, jnp.int32).astype(f32)
+    source, keep = [], []
+    for slot in range(capacity):
+        at, found = zero, zero
+        for m in range(members):
+            hit = dest[m] * pair + rank[m] == slot
+            at = at + jnp.where(hit, jnp.int32(m), zero)
+            found = found + jnp.where(hit, one, zero)
+        source.append(at)
+        keep.append(found)
 
     barrier = pltpu.get_barrier_semaphore()
 
@@ -198,22 +240,57 @@
             )
         )
 
-    def send_state(l):
+    def send_state(step):
+        l, c = steps[step]
         copies = []
         for d in range(1, heads_n):
             h_to = lax.rem(h_me + d, heads_n)
             copies.append(
                 remote(
-                    state_hbm.at[l, 0, 0, pl.ds(h_to * head_dev, head_dev)],
-                    state[l].at[h_me],
-                    state_ssem.at[l, d],
-                    state_rsem.at[l, d],
+                    state_hbm.at[l, 0, 0, pl.ds(h_to * head_dev + c * group_heads, group_heads)],
+                    state[l][c].at[h_me],
+                    state_ssem.at[step, d],
+                    state_rsem.at[step, d],
                     {"heads": h_to},
                 )
             )
         return copies
 
-    state_copies = {0: send_state(0)}
+    ahead = 3
+    state_copies = {i: send_state(i) for i in range(min(ahead, len(steps)))}
+    out_copies = []
+    pumped = [0]
+
+    def pump(upto):
+        while pumped[0] < min(upto, len(steps)):
+            step = pumped[0]
+            pumped[0] += 1
+            l, c = steps[step]
+            own_load[step].wait()
+            for copy in state_copies[step]:
+                copy.wait_recv()
+            if step + ahead < len(steps):
+                state_copies[step + ahead] = send_state(step + ahead)
+            heads = pl.ds(c * group_heads, group_heads)
+            for slot in range(capacity):
+                outbox[l, c, slot // pair, slot % pair] = state[l][c][source[slot]]
+            place = raw_hbm.at[l, 0, pl.ds(s_me * pair, pair), heads]
+            for d in range(1, seq_n):
+                s_to = lax.rem(s_me + d, seq_n)
+                out_copies.append(
+                    remote(
+                        outbox.at[l, c, s_to],
+                        place,
+                        out_ssem.at[step, d],
+                        out_rsem.at[step, d],
+                        {"seq": s_to},
+                    )
+                )
+            own = pltpu.make_async_copy(
+                outbox.at[l, c, s_me], place, local_sem.at[2 * layers + 2 + len(steps) + step]
+            )
+            own.start()
+            loads.append(own)
 
     hid_in[me] = hidden_ref[s_me]
     rows_in[s_me] = rows_ref[...]
@@ -243,9 +320,6 @@
 
     block = 256 if channels % 256 == 0 else channels
     block_out = 256 if width % 256 == 0 else width
-    group_heads = 4 if head_dev % 4 == 0 else head_dev
-    group_rows = group_heads * head_width
-
     for l in range(layers):
         hidden = jnp.concatenate([current[c] for c in range(heads_n)], axis=0).astype(bf16)
         for k in range(width // 128):
@@ -268,7 +342,9 @@
         if l == 0:
             wstep_load.wait()
             wmat_load.wait()
-        step_part = jnp.dot(hidden, wstep[l], preferred_element_type=f32)
+        step_part = lax.dot_general(
+            hidden, wstep[l], (((1,), (1,)), ((), ())), preferred_element_type=f32
+        )
         mat_part = jnp.dot(hidden, wmat[l], preferred_element_type=f32)
         for q in range(seq_n):
             rows = slice(q * members, (q + 1) * members)
@@ -297,6 +373,7 @@
                     {"seq": s_to},
                 )
             )
+        pump(l * chunks + (2 if l == 0 else chunks - 1))
         if l == 0:
             for copy in tail_copies + row_copies:
                 copy.wait_recv()
@@ -323,42 +400,31 @@
         step_in = sm_sum[:, 256 : 256 + head_dev] + sbias_ref[l : l + 1, :]
         step = jnp.maximum(step_in, 0.0) + jnp.log1p(jnp.exp(-jnp.abs(step_in)))
         decay = jnp.exp(-jnp.exp(dlog_ref[l : l + 1, :]) * step)
-        flip_a[0:members, 0:channels] = per_channel(decay)
-        flip_b[0:members, 0:channels] = per_channel(step) * conv_x
+        decay_ch = per_channel(decay)
+        fresh_ch = per_channel(step) * conv_x
         skip = per_channel(jnp.broadcast_to(skip_ref[l : l + 1, :], (8, head_dev)))[0:1]
-        for k in range(channels_pad // 128):
-            cols = slice(k * 128, (k + 1) * 128)
-            col_a[cols, :] = flip_a[:, cols].T
-            col_b[cols, :] = flip_b[:, cols].T
-
-        own_load[l].wait()
-        for copy in state_copies[l]:
-            copy.wait_recv()
-        if l + 1 < layers:
-            state_copies[l + 1] = send_state(l + 1)
-
+        in_m, out_m = conv_m[:, 0:half_m], conv_m[:, half_m:]
+        for m in range(members):
+            vec_rows[l, m, 0:1, :] = decay_ch[m : m + 1]
+            vec_rows[l, m, 1:2, :] = fresh_ch[m : m + 1]
+            vec_rows[l, m, 2:3, 0:half_m] = in_m[m : m + 1]
+
+        pump((l + 1) * chunks)
         lane = lax.broadcasted_iota(jnp.int32, (group_rows, 128), 1)
-
-        @pl.loop(0, head_dev // group_heads)
-        def _(i):
-            rows = pl.ds(pl.multiple_of(i * group_rows, 8), group_rows)
-            heads = pl.ds(i * group_heads, group_heads)
+        for c in range(chunks):
             total = jnp.zeros((group_rows, 128), f32)
             for m in range(members):
-                old = state[l][m, heads].reshape(group_rows, half_m).astype(f32)
-                fresh = (
-                    col_a[rows, m : m + 1] * old
-                    + col_b[rows, m : m + 1] * conv_m[m : m + 1, 0:half_m]
-                )
-                read = jnp.sum(fresh * conv_m[m : m + 1, half_m:], axis=1, keepdims=True)
+                old = state[l][c][m].reshape(group_rows, half_m).astype(f32)
+                read = jnp.sum(old * out_m[m : m + 1], axis=1, keepdims=True)
                 total = jnp.where(lane == m, read, total)
-                state[l][m, heads] = fresh.astype(bf16).reshape(group_heads, head_width, half_m)
-            col_y[rows, :] = total
+            col_y[c * group_rows : (c + 1) * group_rows, :] = total
 
         for k in range(channels_pad // 128):
             cols = slice(k * 128, (k + 1) * 128)
             flip_a[:, cols] = col_y[cols, :].T
-        gated = (flip_a[0:members, 0:channels] + skip * conv_x) * silu(gate)
+        both = jnp.sum(in_m * out_m, axis=1, keepdims=True)
+        read_out = decay_ch * flip_a[0:members, 0:channels] + fresh_ch * both
+        gated = (read_out + skip * conv_x) * silu(gate)
         gated_send[l] = gated
         gated_all[l, s_me] = gated
         square = jnp.broadcast_to(jnp.sum(gated * gated, axis=1, keepdims=True), (members, 128))
@@ -390,37 +456,31 @@
         def _(offset):
             square_copy(offset).start()
 
-        def send_rows():
-            @pl.loop(0, seq_n * pair)
-            def _(slot):
-                source = select_ref[0, slot]
-                keep = select_ref[1, slot].astype(f32).astype(bf16)
-                q_to = slot // pair
-                k_to = lax.rem(slot, pair)
-
-                @pl.loop(0, head_dev // group_heads)
-                def _(i):
-                    heads = pl.ds(i * group_heads, group_heads)
-                    outbox[l, q_to, k_to, heads] = state[l][source, heads] * keep
-
-            for d in range(1, seq_n):
-                s_to = lax.rem(s_me + d, seq_n)
+        for slot in range(capacity):
+            vec_send[l, slot // pair, slot % pair] = vec_rows[l, source[slot]] * keep[slot].astype(
+                f32
+            )
+        for d in range(1, seq_n):
+            s_to = lax.rem(s_me + d, seq_n)
+            out_copies.append(
                 remote(
-                    outbox.at[l, s_to],
-                    newstate_hbm.at[l, 0, pl.ds(s_me * pair, pair)],
-                    out_ssem.at[l, d],
-                    out_rsem.at[l, d],
+                    vec_send.at[l, s_to],
+                    vec_hbm.at[l, pl.ds(s_me * pair, pair)],
+                    vec_ssem.at[l, d],
+                    vec_rsem.at[l, d],
                     {"seq": s_to},
                 )
-            own = pltpu.make_async_copy(
-                outbox.at[l, s_me],
-                newstate_hbm.at[l, 0, pl.ds(s_me * pair, pair)],
-                local_sem.at[3 * layers + 2 + l],
-            )
-            own.start()
-            loads.append(own)
-
-        send_rows()
+            )
+        own = pltpu.make_async_copy(
+            vec_send.at[l, s_me],
+            vec_hbm.at[l, pl.ds(s_me * pair, pair)],
+            local_sem.at[2 * layers + 2 + 2 * len(steps) + l],
+        )
+        own.start()
+        loads.append(own)
+
+        if l + 1 < layers:
+            pump((l + 1) * chunks + 1)
 
         for copy in g_copies:
             copy.wait_recv()
@@ -489,8 +549,7 @@
         if l + 1 < layers:
             for c in range(heads_n):
                 current[c] = current_next[c]
-            if l == 0:
-                pass
+            pump((l + 1) * chunks + chunks // 2)
 
     final = jnp.concatenate([result_send[layers - 1, c] for c in range(heads_n)], axis=0)
     targets = jnp.concatenate([rows_in[q] for q in range(seq_n)], axis=0)
@@ -511,18 +570,31 @@
         copy.wait()
     for copy in pending:
         copy.wait_send()
-    for l in range(layers):
-        for d in range(1, seq_n):
-            pltpu.make_async_remote_copy(
-                src_ref=outbox.at[l, s_me],
-                dst_ref=newstate_hbm.at[
-                    l, 0, pl.ds(lax.rem(s_me + seq_n - d, seq_n) * pair, pair)
-                ],
-                send_sem=out_ssem.at[l, d],
-                recv_sem=out_rsem.at[l, d],
-                device_id={"seq": lax.rem(s_me + d, seq_n)},
-                device_id_type=MESH,
-            ).wait_recv()
+    for copy in out_copies:
+        copy.wait_recv()
+
+
+def update_kernel(dims, vec_ref, raw_ref, given_ref, new_ref, decoded_ref, flip, cols):
+    capacity, group_rows, state_width, channels = dims
+    at = pl.program_id(1)
+
+    @pl.when(at == 0)
+    def _():
+        decoded_ref[...] = given_ref[...]
+        for r in range(capacity):
+            flip[r : r + 1, 0:channels] = vec_ref[0, r, 0:1, :]
+            flip[capacity + r : capacity + r + 1, 0:channels] = vec_ref[0, r, 1:2, :]
+        for k in range(flip.shape[1] // 128):
+            part = slice(k * 128, (k + 1) * 128)
+            cols[part, :] = flip[:, part].T
+
+    rows = pl.ds(pl.multiple_of(at * group_rows, 8), group_rows)
+    for r in range(capacity):
+        old = raw_ref[0, 0, r].reshape(group_rows, state_width).astype(f32)
+        fresh = cols[rows, r : r + 1] * old + (
+            cols[rows, capacity + r : capacity + r + 1] * vec_ref[0, r, 2:3, 0:state_width]
+        )
+        new_ref[0, 0, r] = fresh.astype(bf16).reshape(new_ref.shape[3:])
 
 
 def on_device(
@@ -560,23 +632,13 @@
     tail_rows = layers * (taps - 1)
     devices = seq_n * heads_n
 
-    dest = decode_group[:, 0]
-    member_ids = jnp.arange(members, dtype=jnp.int32)
-    earlier = (dest[:, None] == dest[None, :]) & (member_ids[None, :] < member_ids[:, None])
-    rank = jnp.sum(earlier.astype(jnp.int32), axis=1)
-    target = dest * pair + rank
-    matches = target[None, :] == jnp.arange(capacity, dtype=jnp.int32)[:, None]
-    source = jnp.sum(jnp.where(matches, member_ids[None, :], 0), axis=1)
-    filled = jnp.sum(matches.astype(jnp.int32), axis=1)
-    select = jnp.stack([source, filled])
-    row = dest * capacity + lax.axis_index("seq") * pair + rank
-    rows = jnp.broadcast_to(row.astype(f32)[:, None], (members, 128))
-
-    tails = jnp.transpose(
-        channel_tail.reshape(tail_rows, heads_n, channels), (1, 0, 2)
-    ).astype(f32)
-    mtails = matrix_tail.reshape(tail_rows, 2 * state_width).astype(f32)
-    hidden = last_hidden.reshape(seq_n, 1, width).astype(f32)
+    group_heads = 4 if head_dev % 4 == 0 else head_dev
+    chunks = head_dev // group_heads
+    steps = layers * chunks
+    groups = decode_group.reshape(members)
+    tails = jnp.transpose(channel_tail.reshape(layers, taps - 1, model_width), (1, 0, 2))
+    mtails = jnp.transpose(matrix_tail.reshape(layers, taps - 1, 2 * state_width), (1, 0, 2))
+    hidden = last_hidden.reshape(seq_n, 1, width)
 
     dims = (
         layers, heads_n, seq_n, members, head_dev, head_width, width, channels, pair, taps
@@ -589,9 +651,9 @@
     scratch = [
         V((layers, width, 2, channels), bf16),
         V((layers, channels, width), bf16),
-        V((layers, width, head_dev), bf16),
+        V((layers, head_dev, width), bf16),
         V((layers, width, 2 * state_width), bf16),
-        V((layers, seq_n, pair, head_dev, head_width, state_width), bf16),
+        V((layers, chunks, seq_n, pair, group_heads, head_width, state_width), bf16),
         V((requests, 1, width), f32),
         V((heads_n, tail_rows, channels), f32),
         V((heads_n, tail_rows, 2 * state_width), f32),
@@ -606,10 +668,13 @@
         V((layers, seq_n, members, 384), f32),
         V((layers, seq_n, members, 384), f32),
         V((128, channels_pad), f32),
-        V((128, channels_pad), f32),
         V((channels_pad, 128), f32),
-        V((channels_pad, 128), f32),
-        V((channels_pad, 128), f32),
+        V((heads_n, tail_rows, channels), f32),
+        V((tail_rows, 2 * state_width), f32),
+        V((seq_n, 1, width), f32),
+        V((members, 128), f32),
+        V((layers, members, 3, channels), f32),
+        V((layers, seq_n, pair, 3, channels), f32),
         V((layers, seq_n, members, channels), f32),
         V((layers, members, channels), f32),
         V((layers, devices, members, 128), f32),
@@ -617,9 +682,9 @@
         V((layers, heads_n, chunk_rows, width), f32),
         V((layers, heads_n, chunk_rows, width), f32),
         V((layers, heads_n, chunk_rows, width), f32),
-        dma((4 * layers + 2,)),
-        dma((layers, heads_n)),
-        dma((layers, heads_n)),
+        dma((3 * layers + 2 + 2 * steps,)),
+        dma((steps, heads_n)),
+        dma((steps, heads_n)),
         dma((devices,)),
         dma((devices,)),
         dma((seq_n,)),
@@ -640,22 +705,25 @@
         dma((layers, heads_n)),
         dma((layers, heads_n)),
         dma((layers, heads_n)),
+        dma((steps, seq_n)),
+        dma((steps, seq_n)),
         dma((layers, seq_n)),
         dma((layers, seq_n)),
-    ] + [V((members, head_dev, head_width, state_width), bf16) for _ in range(layers)]
-    decoded, new_state = pl.pallas_call(
+    ] + [V((members, group_heads, head_width, state_width), bf16) for _ in range(steps)]
+    decoded, raw, vectors = pl.pallas_call(
         functools.partial(kernel, dims),
         out_shape=(
             jax.ShapeDtypeStruct((share_rows, width), bf16),
             jax.ShapeDtypeStruct(
                 (layers, 1, capacity, head_dev, head_width, state_width), bf16
             ),
+            jax.ShapeDtypeStruct((layers, capacity, 3, channels), f32),
         ),
         in_specs=[
-            smem, anyw, vmem, vmem, vmem, vmem, anyw, anyw, anyw,
+            smem, anyw, vmem, vmem, vmem, anyw, anyw, anyw,
             vmem, vmem, vmem, vmem, vmem, vmem, anyw,
         ],
-        out_specs=(vmem, anyw),
+        out_specs=(vmem, anyw, anyw),
         scratch_shapes=scratch,
         compiler_params=pltpu.CompilerParams(
             collective_id=0, has_side_effects=True, vmem_limit_bytes=58 * 1024 * 1024
@@ -667,14 +735,13 @@
         ),
         name="handover",
     )(
-        select,
+        groups,
         final_state,
         tails,
         mtails,
         hidden,
-        rows,
         input_weight,
-        step_weight,
+        jnp.swapaxes(step_weight, 1, 2),
         matrix_weight,
         channel_conv,
         matrix_conv,
@@ -684,6 +751,29 @@
         norm_gain,
         output_weight,
     )
+    block = (1, 1, capacity, group_heads, head_width, state_width)
+    new_state, decoded = pl.pallas_call(
+        functools.partial(
+            update_kernel, (capacity, group_heads * head_width, state_width, channels)
+        ),
+        grid=(layers, chunks),
+        out_shape=(
+            jax.ShapeDtypeStruct(raw.shape, bf16),
+            jax.ShapeDtypeStruct(decoded.shape, bf16),
+        ),
+        in_specs=[
+            pl.BlockSpec((1, capacity, 3, channels), lambda l, c: (l, 0, 0, 0)),
+            pl.BlockSpec(block, lambda l, c: (l, 0, 0, c, 0, 0)),
+            pl.BlockSpec((share_rows, width), lambda l, c: (0, 0)),
+        ],
+        out_specs=(
+            pl.BlockSpec(block, lambda l, c: (l, 0, 0, c, 0, 0)),
+            pl.BlockSpec((share_rows, width), lambda l, c: (0, 0)),
+        ),
+        scratch_shapes=[V((128, channels_pad), f32), V((channels_pad, 128), f32)],
+        compiler_params=pltpu.CompilerParams(vmem_limit_bytes=32 * 1024 * 1024),
+        name="update",
+    )(vectors, raw, decoded)
     return decoded, new_state
 
 

time: 143 us -> 130 us (0.909)
  local copies, waits for them, and re-layouts: 12.9 us -> 4.18 us
  other arithmetic: 4.22 us -> 0 us
    pallas_call x0 -> x1, Pallas kernels: none -> 8.05 us  [on_device(): pl.pallas_call(functools.partial(update_kernel, (capacity, group_heads *...]
    pallas_call x1, Pallas kernels: 124 us -> 117 us  [on_device(): pl.pallas_call(functools.partial(kernel, dims), out_shape=(jax.ShapeDtype...]
    unnamed x3 -> x6, local copies, waits for them, and re-layouts: 9.27 us -> 4.18 us
    convert_element_type x5 -> x0, local copies, waits for them, and re-layouts: 2.94 us -> none  [the longest x3 1.65 us: on_device(): tails = jnp.transpose(channel_tail.reshape(tail_rows, heads_n, channels),...]
where the time goes in v2:
time: 130 us; the launch traced here: 129 us
  Pallas kernels  125 us (96%)
  local copies, waits for them, and re-layouts  4.18 us (3%)
    pallas_call x1, Pallas kernels, on_device(): pl.pallas_call(functools.partial(kernel, dims), out_shape=(jax.ShapeDtype...  117 us
    pallas_call x1, Pallas kernels, on_device(): pl.pallas_call(functools.partial(update_kernel, (capacity, group_heads *...  8.05 us
    unnamed x6, local copies, waits for them, and re-layouts  4.18 us

profile of v2, /device:TPU:0, one launch (start us, length us, event | category | flops | bytes accessed | tf_op | source)
XLA Modules:
  0.0 129.5 jit_solution(8288087537848994395)
XLA Ops:
  0.6 116.6 %handover.1 = (bf16[8,1280]{1,0:T(8,128)(2,1)}, bf16[2,1,8,16,80,128]{5,4,3,2,1,0:T(8,128)(2,1)}, f32[2,8,3,1280]{3,2,1,0:T(4,128)}) custom-call(s32[4]{0:T(128)} %bitcast.13, bf16[2,1,1,64,80,128]{5,4,3,2,1,0:T(8,128)(2,1)} %state_hbm.1, bf16[3,2,5120]{2,1,0:T(2,128)(2,1)} %bitcast.10, bf16[3,2,256]{2,1,0:T(2,128)(2,1)} %bitcast.12, ...), custom_call_target="tpu_custom_call" | custom-call | flops 629145600 | bytes 30000000 | tf_op jit(solution)/shard_map/handover/pallas_call | solution.py:713
  117.2 0.0 copy-start
  117.2 2.5 %copy-done = bf16[2,1,8,16,80,128]{5,4,3,2,1,0:T(8,128)(2,1)S(1)} copy-done((bf16[2,1,8,16,80,128]{5,4,3,2,1,0:T(8,128)(2,1)S(1)}, bf16[2,1,8,16,80,128]{5,4,3,2,1,0:T(8,128)(2,1)}, u32[]{:S(2)}) %copy-start) | copy-done | bytes 5242904
  119.7 0.0 copy-start.1
  119.7 1.0 copy-done.1
  120.7 0.0 copy-start.2
  120.7 0.7 copy-done.2
  121.4 8.0 %update.1 = (bf16[2,1,8,16,80,128]{5,4,3,2,1,0:T(8,128)(2,1)}, bf16[8,1280]{1,0:T(8,128)(2,1)}) custom-call(f32[2,8,3,1280]{3,2,1,0:T(4,128)S(1)} %copy-done.1, bf16[2,1,8,16,80,128]{5,4,3,2,1,0:T(8,128)(2,1)S(1)} %copy-done, bf16[8,1280]{1,0:T(8,128)(2,1)S(1)} %copy-done.2), custom_call_target="tpu_custom_call" | custom-call | tf_op jit(solution)/shard_map/update/pallas_call | solution.py:755
Async XLA Ops:
  117.2 2.5 %copy-start = (bf16[2,1,8,16,80,128]{5,4,3,2,1,0:T(8,128)(2,1)S(1)}, bf16[2,1,8,16,80,128]{5,4,3,2,1,0:T(8,128)(2,1)}, u32[]{:S(2)}) copy-start(bf16[2,1,8,16,80,128]{5,4,3,2,1,0:T(8,128)(2,1)} %get-tuple-element.8.raw_ref) | copy-start | bytes 15728644
  119.7 1.0 copy-start.1
  120.7 0.7 copy-start.2

commit v3 on v2

--- a/solution.py
+++ b/solution.py
@@ -256,7 +256,7 @@
             )
         return copies
 
-    ahead = 3
+    ahead = 2
     state_copies = {i: send_state(i) for i in range(min(ahead, len(steps)))}
     out_copies = []
     pumped = [0]
@@ -373,7 +373,7 @@
                     {"seq": s_to},
                 )
             )
-        pump(l * chunks + (2 if l == 0 else chunks - 1))
+        pump(2 if l == 0 else (l + 1) * chunks)
         if l == 0:
             for copy in tail_copies + row_copies:
                 copy.wait_recv()
@@ -480,7 +480,7 @@
         loads.append(own)
 
         if l + 1 < layers:
-            pump((l + 1) * chunks + 1)
+            pump((l + 1) * chunks + 2)
 
         for copy in g_copies:
             copy.wait_recv()
@@ -549,7 +549,7 @@
         if l + 1 < layers:
             for c in range(heads_n):
                 current[c] = current_next[c]
-            pump((l + 1) * chunks + chunks // 2)
+            pump((l + 1) * chunks + chunks - 1)
 
     final = jnp.concatenate([result_send[layers - 1, c] for c in range(heads_n)], axis=0)
     targets = jnp.concatenate([rows_in[q] for q in range(seq_n)], axis=0)

time: 130 us -> 123 us (0.946)
  Pallas kernels: 125 us -> 117 us
    pallas_call x1, Pallas kernels: 117 us -> 109 us  [on_device(): pl.pallas_call(functools.partial(kernel, dims), out_shape=(jax.ShapeDtype...]
where the time goes in v3:
time: 123 us; the launch traced here: 122 us
  Pallas kernels  117 us (95%)
  local copies, waits for them, and re-layouts  4.18 us (3%)
    pallas_call x1, Pallas kernels, on_device(): pl.pallas_call(functools.partial(kernel, dims), out_shape=(jax.ShapeDtype...  109 us
    pallas_call x1, Pallas kernels, on_device(): pl.pallas_call(functools.partial(update_kernel, (capacity, group_heads *...  8.05 us
    unnamed x6, local copies, waits for them, and re-layouts  4.18 us

profile of v3, /device:TPU:0, one launch (start us, length us, event | category | flops | bytes accessed | tf_op | source)
XLA Modules:
  0.0 122.2 jit_solution(10471254418131030306)
XLA Ops:
  0.6 109.3 %handover.1 = (bf16[8,1280]{1,0:T(8,128)(2,1)}, bf16[2,1,8,16,80,128]{5,4,3,2,1,0:T(8,128)(2,1)}, f32[2,8,3,1280]{3,2,1,0:T(4,128)}) custom-call(s32[4]{0:T(128)} %bitcast.13, bf16[2,1,1,64,80,128]{5,4,3,2,1,0:T(8,128)(2,1)} %state_hbm.1, bf16[3,2,5120]{2,1,0:T(2,128)(2,1)} %bitcast.10, bf16[3,2,256]{2,1,0:T(2,128)(2,1)} %bitcast.12, ...), custom_call_target="tpu_custom_call" | custom-call | flops 629145600 | bytes 30000000 | tf_op jit(solution)/shard_map/handover/pallas_call | solution.py:713
  110.0 0.0 copy-start
  110.0 2.5 %copy-done = bf16[2,1,8,16,80,128]{5,4,3,2,1,0:T(8,128)(2,1)S(1)} copy-done((bf16[2,1,8,16,80,128]{5,4,3,2,1,0:T(8,128)(2,1)S(1)}, bf16[2,1,8,16,80,128]{5,4,3,2,1,0:T(8,128)(2,1)}, u32[]{:S(2)}) %copy-start) | copy-done | bytes 5242904
  112.5 0.0 copy-start.1
  112.5 1.0 copy-done.1
  113.4 0.0 copy-start.2
  113.4 0.7 copy-done.2
  114.2 8.0 %update.1 = (bf16[2,1,8,16,80,128]{5,4,3,2,1,0:T(8,128)(2,1)}, bf16[8,1280]{1,0:T(8,128)(2,1)}) custom-call(f32[2,8,3,1280]{3,2,1,0:T(4,128)S(1)} %copy-done.1, bf16[2,1,8,16,80,128]{5,4,3,2,1,0:T(8,128)(2,1)S(1)} %copy-done, bf16[8,1280]{1,0:T(8,128)(2,1)S(1)} %copy-done.2), custom_call_target="tpu_custom_call" | custom-call | tf_op jit(solution)/shard_map/update/pallas_call | solution.py:755
Async XLA Ops:
  110.0 2.5 %copy-start = (bf16[2,1,8,16,80,128]{5,4,3,2,1,0:T(8,128)(2,1)S(1)}, bf16[2,1,8,16,80,128]{5,4,3,2,1,0:T(8,128)(2,1)}, u32[]{:S(2)}) copy-start(bf16[2,1,8,16,80,128]{5,4,3,2,1,0:T(8,128)(2,1)} %get-tuple-element.8.raw_ref) | copy-start | bytes 15728644
  112.5 1.0 copy-start.1
  113.4 0.7 copy-start.2
